TPU v7x, 32 devices: a whole 2x2x4 slice. The times are simulated.
32 devices in a mesh: dp: 4 (over z), row: 4 (over y, x), col: 2 (over core).
Axes of the slice: x: 2, y: 2, z: 4, core: 2. Of those that a mesh axis runs over, the one named last changes fastest.
Arguments:
- layer_input: bfloat16 [768, 4096], P(('dp', 'col'), 'row'), may hold values from -6 to 6
- hidden_grad: bfloat16 [768, 14336], P(('dp', 'row'), 'col'), may hold values from -6 to 6
- gate_slots: bfloat16 [4, 2, 192, 128, 128], P('row', 'col', 'dp'), may hold values from -0.125 to 0.125
- up_slots: bfloat16 [4, 2, 192, 128, 128], P('row', 'col', 'dp'), may hold values from -0.125 to 0.125
- block_mask: int32 [32, 112], replicated, may hold values from 0 to 1, as said below
Outputs:
- input_grad: bfloat16 [768, 4096], P(('dp', 'col'), 'row')
- gate_slot_grad: float32 [4, 2, 192, 128, 128], P('row', 'col', 'dp')
- up_slot_grad: float32 [4, 2, 192, 128, 128], P('row', 'col', 'dp')
Inputs may be any that keep to these rules, and one draw needn't show every extreme that they name: `block_mask`: every tile of 8 x 56 blocks keeps between 96 and 192 blocks; some tile keeps exactly 192, which tile depends on the draw.
All inputs are finite; a program needn't handle non-finite values.
Results may differ from a plain program's by a relative error of at most 0.022.
Values may be sent and summed in bfloat16 or wider, within the bound.
A program may use at most 128 MiB of HBM per device.

v0:
```python
import jax
import jax.numpy as jnp
from jax import lax
from jax.sharding import PartitionSpec as P


def slot_maps(block_mask, tile_rows, tile_cols, capacity):
    row_first = lax.axis_index("row") * tile_rows
    col_first = lax.axis_index("col") * tile_cols
    tile_mask = lax.dynamic_slice(block_mask, (row_first, col_first), (tile_rows, tile_cols))
    flat_mask = tile_mask.reshape(tile_rows * tile_cols)
    position = jnp.cumsum(flat_mask) - 1
    slot_ids = jnp.arange(capacity, dtype=jnp.int32)
    chosen = ((flat_mask[:, None] > 0) & (position[:, None] == slot_ids[None, :])).astype(jnp.int32)
    block_ids = jnp.arange(tile_rows * tile_cols, dtype=jnp.int32)
    slot_block = jnp.sum(chosen * block_ids[:, None], axis=0)
    live_slots = jnp.sum(chosen, axis=0).astype(jnp.float32)
    slot_row = slot_block // tile_cols
    slot_col = slot_block % tile_cols
    col_table = (slot_col[:, None] == jnp.arange(tile_cols, dtype=jnp.int32)[None, :]).astype(
        jnp.float32
    ) * live_slots[:, None]
    row_table = (slot_row[:, None] == jnp.arange(tile_rows, dtype=jnp.int32)[None, :]).astype(
        jnp.float32
    ) * live_slots[:, None]
    return (slot_row, slot_col, live_slots, col_table, row_table)


def slot_products(picked, pair_weights, col_table):
    per_slot = jnp.einsum("tsk,skn->tsn", picked, pair_weights, preferred_element_type=jnp.float32)
    return jnp.einsum("tsn,sc->tcn", per_slot, col_table, precision=lax.Precision.HIGHEST)


def back_products(grad_picked, pair_weights, row_table):
    per_slot = jnp.einsum(
        "tsn,skn->tsk", grad_picked, pair_weights, preferred_element_type=jnp.float32
    )
    return jnp.einsum("tsk,sr->trk", per_slot, row_table, precision=lax.Precision.HIGHEST)


def on_device(layer_input, hidden_grad, gate_slots, up_slots, block_mask):
    gate_local = gate_slots[0, 0]
    up_local = up_slots[0, 0]
    block_size = gate_local.shape[-1]
    replicas = lax.axis_size("dp")
    capacity = gate_local.shape[0] * replicas
    token_panel = lax.all_gather(layer_input, "col", axis=0, tiled=True)
    grad_panel = lax.all_gather(hidden_grad, "row", axis=0, tiled=True)
    tok_rows = token_panel.shape[0]
    feat_cols = token_panel.shape[1]
    unit_cols = grad_panel.shape[1]
    tile_rows = feat_cols // block_size
    tile_cols = unit_cols // block_size
    slot_row, slot_col, live_slots, col_table, row_table = slot_maps(
        block_mask, tile_rows, tile_cols, capacity
    )
    token_blocks = token_panel.reshape(tok_rows, tile_rows, block_size)
    picked_tokens = jnp.take(token_blocks, slot_row, axis=1)
    gate_all, up_all = (
        lax.all_gather(gate_local, "dp", axis=0, tiled=True),
        lax.all_gather(up_local, "dp", axis=0, tiled=True),
    )
    pair_all = jnp.concatenate([gate_all, up_all], axis=2)
    pair_part = slot_products(picked_tokens, pair_all, col_table)
    gate_part = pair_part[:, :, :block_size].reshape(tok_rows, unit_cols)
    up_part = pair_part[:, :, block_size:].reshape(tok_rows, unit_cols)
    gate_sum, up_sum = (
        lax.psum(gate_part.astype(jnp.bfloat16), "row").astype(jnp.float32),
        lax.psum(up_part.astype(jnp.bfloat16), "row").astype(jnp.float32),
    )
    sigmoid_gate = jax.nn.sigmoid(gate_sum)
    upstream = grad_panel.astype(jnp.float32)
    gate_grad = (upstream * up_sum * sigmoid_gate * (1.0 + gate_sum * (1.0 - sigmoid_gate))).astype(
        jnp.bfloat16
    )
    up_grad = (upstream * gate_sum * sigmoid_gate).astype(jnp.bfloat16)
    grad_pair = jnp.concatenate(
        [
            gate_grad.reshape(tok_rows, tile_cols, block_size),
            up_grad.reshape(tok_rows, tile_cols, block_size),
        ],
        axis=2,
    )
    grad_picked = jnp.take(grad_pair, slot_col, axis=1)
    summed = back_products(grad_picked, pair_all, row_table)
    input_sum = lax.psum_scatter(
        summed.reshape(tok_rows // lax.axis_size("col") * lax.axis_size("col"), feat_cols).astype(
            jnp.bfloat16
        ),
        "col",
        scatter_dimension=0,
        tiled=True,
    )
    pair_term = (
        jnp.einsum("tsk,tsn->skn", picked_tokens, grad_picked, preferred_element_type=jnp.float32)
        * live_slots[:, None, None]
    )
    pair_total = lax.psum_scatter(
        pair_term.astype(jnp.bfloat16), "dp", scatter_dimension=0, tiled=True
    ).astype(jnp.float32)
    gate_out = (pair_total[:, :, :block_size] / replicas)[None, None]
    up_out = (pair_total[:, :, block_size:] / replicas)[None, None]
    return (input_sum, gate_out, up_out)


def solution(mesh):
    return jax.shard_map(
        on_device,
        mesh=mesh,
        in_specs=(
            P(("dp", "col"), "row"),
            P(("dp", "row"), "col"),
            P("row", "col", "dp", None, None),
            P("row", "col", "dp", None, None),
            P(),
        ),
        out_specs=(
            P(("dp", "col"), "row"),
            P("row", "col", "dp", None, None),
            P("row", "col", "dp", None, None),
        ),
        check_vma=False,
    )
```

profile of v0, /device:TPU:0, one launch (start us, length us, event | category | flops | bytes accessed | tf_op | source)
XLA Modules:
  0.0 728.9 jit_solution(1928009497294840013)
XLA Ops:
  7.9 0.7 all-gather.10.cloned.1.call-update
  9.4 0.8 dynamic_slice.3
  11.2 2.4 all_gather.15
  13.6 9.9 %gather_fusion = bf16[192,192,128]{2,1,0:T(8,128)(2,1)} fusion(bf16[192,8,128]{2,0,1:T(8,128)(2,1)S(1)} %copy_bitcast_fusion.5, s32[1024]{0:T(1024)S(1)} %pad_clamp_fusion.1), kind=kCustom, calls=%fused_computation | custom fusion | bytes 18875136 | tf_op jit(solution)/shard_map/jit(_take)/gather | solution.py:58
  23.6 104.1 %all-gather.8.cloned.1.call-done = bf16[1,1,192,128,128]{4,3,1,0,2:T(8,128)(2,1)} async-done(((bf16[1,1,48,128,128]{4,3,1,0,2:T(8,128)(2,1)}), bf16[1,1,192,128,128]{4,3,1,0,2:T(8,128)(2,1)}) %all-gather.8.cloned.1.call-update) | async-done | bytes 6291472 | tf_op jit(solution)/shard_map/all_gather | solution.py:60
  127.7 115.2 %all-gather.10.cloned.1.call-done = bf16[1,1,192,128,128]{4,3,1,0,2:T(8,128)(2,1)} async-done(((bf16[1,1,48,128,128]{4,3,1,0,2:T(8,128)(2,1)}), bf16[1,1,192,128,128]{4,3,1,0,2:T(8,128)(2,1)}) %all-gather.10.cloned.1.call-update) | async-done | bytes 6291472 | tf_op jit(solution)/shard_map/all_gather | solution.py:61
  242.9 20.1 %convolution_bitcast_fusion = f32[192,192,256]{2,0,1:T(8,128)} fusion(bf16[192,128,128]{2,1,0:T(8,128)(2,1)} %bitcast.76, bf16[192,128,128]{2,1,0:T(8,128)(2,1)} %bitcast.74, bf16[192,192,128]{2,1,0:T(8,128)(2,1)} %gather_fusion, pred[192]{0:T(512)(128)(4,1)S(1)} %get-tuple-element.21), kind=kOutput, calls=%fused_computation.12 | convolution fusion | flops 2445803520 | bytes 59769024 | tf_op jit(solution)/shard_map/tsk,skn->tsn/dot_general | solution.py:30
  262.9 67.1 %convert_bitcast_fusion = bf16[192,56,256]{2,1,0:T(8,128)(2,1)S(1)} fusion(f32[192,192,256]{2,0,1:T(8,128)} %convolution_bitcast_fusion, f32[192]{0:T(256)S(1)} %convert_element_type.55, s32[192]{0:T(256)S(1)} %get-tuple-element.8), kind=kOutput, calls=%fused_computation.32 | convolution fusion | flops 6344561664 | bytes 43255296 | tf_op jit(solution)/shard_map/tsn,sc->tcn/dot_general | solution.py:31
  330.0 0.9 fusion.53
  331.0 3.3 copy_bitcast_fusion
  334.4 124.1 %all-reduce.4.cloned.1.call-done = (bf16[192,7168]{1,0:T(8,128)(2,1)}, bf16[192,7168]{1,0:T(8,128)(2,1)}) async-done(((bf16[192,7168]{1,0:T(8,128)(2,1)}, bf16[192,7168]{1,0:T(8,128)(2,1)}), (bf16[192,7168]{1,0:T(8,128)(2,1)}, bf16[192,7168]{1,0:T(8,128)(2,1)})) %all-reduce.4.cloned.1.call-update) | async-done | bytes 5505040 | tf_op jit(solution)/shard_map/psum | solution.py:68
  458.5 5.2 fusion.31
  463.7 0.8 copy.47
  464.5 0.8 copy.48
  465.3 3.1 pad_maximum_fusion.3
  468.4 12.9 %gather_fusion.1 = bf16[192,192,256]{2,1,0:T(8,128)(2,1)} fusion(bf16[192,56,256]{2,0,1:T(8,128)(2,1)} %pad_maximum_fusion.3, s32[1024]{0:T(1024)S(1)} %pad_clamp_fusion), kind=kCustom, calls=%fused_computation.1 | custom fusion | bytes 37749504 | tf_op jit(solution)/shard_map/jit(_take)/gather | solution.py:84
  481.3 17.1 %multiply_convert_fusion = bf16[192,128,256]{2,1,0:T(8,128)(2,1)} fusion(f32[192]{0:T(256)S(1)} %convert_element_type.55, bf16[192,192,256]{2,1,0:T(8,128)(2,1)} %gather_fusion.1, pred[192]{0:T(512)(128)(4,1)S(1)} %get-tuple-element.7, bf16[192,192,128]{2,1,0:T(8,128)(2,1)} %gather_fusion, pred[192]{0:T(512)(128)(4,1)S(1)} %get-tuple-element.21), kind=kOutput, calls=%fused_computation.4 | convolution fusion | flops 2442657792 | bytes 40895616 | tf_op jit(solution)/shard_map/tsk,tsn->skn/dot_general | solution.py:95
  498.4 19.7 %fusion.10 = f32[192,192,128]{2,0,1:T(8,128)} fusion(bf16[192,128,128]{2,1,0:T(8,128)(2,1)} %bitcast.77, bf16[192,128,128]{2,1,0:T(8,128)(2,1)} %bitcast.75, bf16[192,192,256]{2,1,0:T(8,128)(2,1)} %gather_fusion.1, pred[192]{0:T(512)(128)(4,1)S(1)} %get-tuple-element.7), kind=kOutput, calls=%fused_computation.17 | convolution fusion | flops 2450522112 | bytes 50331840 | tf_op jit(solution)/shard_map/tsn,skn->tsk/dot_general | solution.py:35
  518.1 30.5 %fusion.32 = bf16[8,192,128]{2,0,1:T(8,128)(2,1)S(1)} fusion(f32[192,192,128]{2,0,1:T(8,128)} %fusion.10, f32[192]{0:T(256)S(1)} %convert_element_type.55, s32[192]{0:T(256)S(1)} %get-tuple-element.22), kind=kOutput, calls=%fused_computation.43 | convolution fusion | flops 453184512 | bytes 19269120 | tf_op jit(solution)/shard_map/tsk,sr->trk/dot_general | solution.py:38
  548.6 0.8 copy.49
  549.4 161.0 %reduce-scatter.5.cloned.1.call-done = bf16[48,128,256]{2,1,0:T(8,128)(2,1)} async-done(((bf16[192,128,256]{2,1,0:T(8,128)(2,1)}), bf16[48,128,256]{2,1,0:T(8,128)(2,1)}) %reduce-scatter.5.cloned.1.call-update) | async-done | bytes 3145744 | tf_op jit(solution)/shard_map/reduce_scatter | solution.py:98
  710.4 2.7 convert_element_type.67
  713.1 3.6 fusion.28
  716.7 5.2 reduce-scatter.3.cloned.1.call-done
  (29 shorter events, 2.7 us)
Async XLA Ops:
  7.2 120.5 %all-gather.8.cloned.1.call-start = ((), (), s32[]{:S(2)}) async-start(), calls=%async_computation.5 | async-start | bytes 7864320 | tf_op jit(solution)/shard_map/all_gather | solution.py:60
  7.9 235.0 %all-gather.10.cloned.1.call-start = ((), (), s32[]{:S(2)}) async-start(), calls=%async_computation.6 | async-start | bytes 7864320 | tf_op jit(solution)/shard_map/all_gather | solution.py:61
  8.6 325.7 %all-gather.6.cloned.1.call-start = ((), (), s32[]{:S(2)}) async-start(), calls=%async_computation.2 | async-start | bytes 3440640 | tf_op jit(solution)/shard_map/all_gather | solution.py:48
  9.4 449.1 %all-reduce.4.cloned.1.call-start = ((), (), s32[]{:S(2)}) async-start(), calls=%async_computation.7 | async-start | bytes 11010048 | tf_op jit(solution)/shard_map/psum | solution.py:68
  334.3 376.1 %reduce-scatter.5.cloned.1.call-start = ((), (), s32[]{:S(2)}) async-start(), calls=%async_computation.4 | async-start | bytes 15728640 | tf_op jit(solution)/shard_map/reduce_scatter | solution.py:98
  498.4 223.5 %reduce-scatter.3.cloned.1.call-start = ((), (), s32[]{:S(2)}) async-start(), calls=%async_computation.3 | async-start | bytes 589824 | tf_op jit(solution)/shard_map/reduce_scatter | solution.py:86
Sparse Core Ops, SparseCore 0:
  9.6 118.0 all-gather.7
  129.3 113.5 all-gather.9
  244.7 38.9 all-gather.5
  334.4 124.0 all-reduce.3
  498.5 211.8 reduce-scatter.4
  713.1 8.7 reduce-scatter.2
where the time goes:
time: 734 us; the launch traced here: 729 us
  waiting for transfers between devices  512 us (70%)
  matrix products  154 us (21%)
  local copies, waits for them, and re-layouts  30.5 us (4%)
  other arithmetic  15.3 us (2%)
  between operations  14.4 us (2%)
    reduce_scatter x1, waiting for transfers between devices, on_device(): lax.psum_scatter(pair_term.astype(jnp.bfloat16), 'dp', scatter_dimension=...  161 us
    psum x1, waiting for transfers between devices, on_device(): lax.psum(gate_part.astype(jnp.bfloat16), 'row').astype(jnp.float32)  124 us
    all_gather x1, waiting for transfers between devices, on_device(): lax.all_gather(up_local, 'dp', axis=0, tiled=True)  115 us
    all_gather x1, waiting for transfers between devices, on_device(): lax.all_gather(gate_local, 'dp', axis=0, tiled=True)  104 us
    dot_general x1, matrix products, slot_products(): jnp.einsum('tsn,sc->tcn', per_slot, col_table, precision=lax.Precision.HI...  67.1 us
    dot_general x1, matrix products, back_products(): jnp.einsum('tsk,sr->trk', per_slot, row_table, precision=lax.Precision.HI...  30.5 us
    dot_general x1, matrix products, slot_products(): jnp.einsum('tsk,skn->tsn', picked, pair_weights, preferred_element_type=j...  20.1 us
    dot_general x1, matrix products, back_products(): jnp.einsum('tsn,skn->tsk', grad_picked, pair_weights, preferred_element_t...  19.7 us
  transfers between devices with their start and end apart: 6, of which 5 were waited for; matrix products, arithmetic and copies ran while one was open for 22% of the time, Pallas kernels for 0%

commit v1 on v0

v1 whole, which is shorter than its diff:
```python
import functools

import jax
import jax.numpy as jnp
from jax import lax
from jax.experimental import pallas as pl
from jax.experimental.pallas import tpu as pltpu
from jax.sharding import PartitionSpec as P

MESH = pl.DeviceIdType.MESH


def slot_maps(block_mask, tile_rows, tile_cols, local_cap):
    row_first = lax.axis_index("row") * tile_rows
    col_first = lax.axis_index("col") * tile_cols
    tile_mask = lax.dynamic_slice(block_mask, (row_first, col_first), (tile_rows, tile_cols))
    blocks = tile_rows * tile_cols
    flat_mask = tile_mask.reshape(blocks)
    ids = jnp.arange(blocks, dtype=jnp.int32)
    before = jnp.sum(jnp.where(ids[None, :] < ids[:, None], flat_mask[None, :], 0), axis=1)
    local = before - lax.axis_index("dp") * local_cap
    here = (flat_mask > 0) & (local >= 0) & (local < local_cap)
    where_slot = jnp.where(here, local, local_cap).astype(jnp.int32)
    slot_ids = jnp.arange(local_cap, dtype=jnp.int32)
    chosen = (where_slot[:, None] == slot_ids[None, :]).astype(jnp.int32)
    slot_block = jnp.sum(chosen * ids[:, None], axis=0)
    live = jnp.sum(chosen, axis=0)
    return where_slot, slot_block // tile_cols, slot_block % tile_cols, live


def kernel(
    sizes, where_ref, tok_ref, w_ref, hg_ref,
    dx_ref, grads_ref,
    grads, part, recv1, recv2, recvz, dense, dx_acc,
    s1, r1, s2, r2, sz, rz, sa, ra, sb, rb, sc, rc, so,
):
    n_row, n_dp, n_chunks, tile_rows, lag, ring, part_ring = sizes
    bs = hg_ref.shape[-1]
    me_row = lax.axis_index("row")
    me_dp = lax.axis_index("dp")
    low, high = me_row % 2, me_row // 2
    px = high * 2 + (1 - low)
    py = (1 - high) * 2 + low
    diag = 3 - me_row

    barrier = pltpu.get_barrier_semaphore()
    for other in (px, py):
        pl.semaphore_signal(barrier, inc=1, device_id={"row": other}, device_id_type=MESH)
    for step in range(1, n_dp):
        pl.semaphore_signal(barrier, inc=1, device_id={"dp": (me_dp + step) % n_dp}, device_id_type=MESH)
    pl.semaphore_wait(barrier, 2 + n_dp - 1)

    def send(src, dst, s, r, device):
        return pltpu.make_async_remote_copy(
            src_ref=src, dst_ref=dst, send_sem=s, recv_sem=r, device_id=device, device_id_type=MESH
        )

    def partners(c):
        q = c % 2
        return q * py + (1 - q) * px, q * px + (1 - q) * py

    def build(c):
        for r in range(tile_rows):
            dense[r * bs : (r + 1) * bs, :] = w_ref[where_ref[r * n_chunks + c]]

    def first_copies(c):
        p1, p2 = partners(c)
        slot, k = c % part_ring, c % ring
        return [
            send(part.at[slot, p1], recv1.at[k, 0], s1.at[k, 0], r1.at[k, 0], {"row": p1}),
            send(part.at[slot, diag], recv1.at[k, 1], s1.at[k, 1], r1.at[k, 1], {"row": p1}),
        ]

    def second_copy(c):
        p1, p2 = partners(c)
        k = c % ring
        return send(recv1.at[k, 1], recv2.at[k], s2.at[k], r2.at[k], {"row": p2})

    def depth_copies(c):
        k = c % ring
        out = []
        for step in range(1, n_dp):
            other = (me_dp + step) % n_dp
            out.append(send(
                recv2.at[k, other], recvz.at[k, step - 1], sz.at[k, step - 1], rz.at[k, step - 1], {"dp": other}
            ))
        return out

    def depth_gathers(c):
        k = c % ring
        mine = grads.at[c, me_row, me_dp]
        return [
            send(mine, mine, sa.at[k, step - 1], ra.at[k, step - 1], {"dp": (me_dp + step) % n_dp})
            for step in range(1, n_dp)
        ]

    def near_gather(c):
        p1, p2 = partners(c)
        k = c % ring
        return send(grads.at[c, me_row], grads.at[c, me_row], sb.at[k], rb.at[k], {"row": p2})

    def far_gathers(c):
        p1, p2 = partners(c)
        k = c % ring
        return [
            send(grads.at[c, me_row], grads.at[c, me_row], sc.at[k, 0], rc.at[k, 0], {"row": p1}),
            send(grads.at[c, p2], grads.at[c, p2], sc.at[k, 1], rc.at[k, 1], {"row": p1}),
        ]

    def keep(c):
        return pltpu.make_async_copy(grads.at[c], grads_ref.at[c], so.at[c])

    dx_acc[...] = jnp.zeros_like(dx_acc)

    def iteration(t, carry):
        def at(stage, body):
            c = t - lag * stage

            @pl.when((c >= 0) & (c < n_chunks))
            def _():
                body(c)

        def stage1(c):
            for copy in first_copies(c):
                copy.wait()
            p1, p2 = partners(c)
            slot, k = c % part_ring, c % ring
            for i, r in ((1, p2), (0, me_row)):
                recv1[k, i] = (
                    part[slot, r].astype(jnp.float32) + recv1[k, i].astype(jnp.float32)
                ).astype(jnp.bfloat16)
                if i == 1:
                    second_copy(c).start()

        def stage2(c):
            second_copy(c).wait()
            k = c % ring
            recv2[k] = (recv1[k, 0].astype(jnp.float32) + recv2[k].astype(jnp.float32)).astype(jnp.bfloat16)
            for copy in depth_copies(c):
                copy.start()

        def stage3(c):
            for copy in depth_copies(c):
                copy.wait()
            k = c % ring
            total = recv2[k, me_dp].astype(jnp.float32)
            for step in range(n_dp - 1):
                total = total + recvz[k, step].astype(jnp.float32)
            gate, up = total[:, :bs], total[:, bs:]
            upstream = hg_ref[c].astype(jnp.float32)
            sig = jax.nn.sigmoid(gate)
            grads[c, me_row, me_dp] = jnp.concatenate(
                [upstream * up * sig * (1.0 + gate * (1.0 - sig)), upstream * gate * sig], axis=1
            ).astype(jnp.bfloat16)
            for copy in depth_gathers(c):
                copy.start()

        def stage4(c):
            for copy in depth_gathers(c):
                copy.wait()
            near_gather(c).start()

        def stage5(c):
            near_gather(c).wait()
            for copy in far_gathers(c):
                copy.start()

        def stage6(c):
            for copy in far_gathers(c):
                copy.wait()
            keep(c).start()
            build(c)

            def rows(r, carry):
                g = grads[c, r].reshape(-1, 2 * bs)
                dx_acc[r] += lax.dot_general(
                    g, dense[...], (((1,), (1,)), ((), ())), preferred_element_type=jnp.float32
                )
                return carry

            lax.fori_loop(0, n_row, rows, 0)

        def stage0(c):
            build(c)
            slot = c % part_ring

            def rows(r, carry):
                part[slot, r] = (
                    jnp.dot(tok_ref[r], dense[...], preferred_element_type=jnp.float32)
                    .astype(jnp.bfloat16)
                    .reshape(part.shape[2:])
                )
                return carry

            lax.fori_loop(0, n_row, rows, 0)
            for copy in first_copies(c):
                copy.start()

        at(5, stage5)
        at(4, stage4)
        at(3, stage3)
        at(2, stage2)
        at(1, stage1)
        at(6, stage6)
        at(0, stage0)
        return carry

    lax.fori_loop(0, n_chunks + 6 * lag, iteration, 0)

    def finish(r, carry):
        dx_ref[r] = dx_acc[r].astype(jnp.bfloat16)
        return carry

    lax.fori_loop(0, n_row, finish, 0)

    def kept(c, carry):
        keep(c).wait()
        return carry

    lax.fori_loop(0, n_chunks, kept, 0)


def slot_kernel(srow_ref, scol_ref, scale_ref, tok_ref, *refs):
    *grad_refs, gate_ref, up_ref = refs
    bs = gate_ref.shape[-1]
    first = pl.program_id(0) * len(grad_refs)
    for i, grad_ref in enumerate(grad_refs):
        total = jnp.dot(tok_ref[srow_ref[first + i]], grad_ref[0], preferred_element_type=jnp.float32)
        total = total * scale_ref[first + i]
        gate_ref[i] = total[:, :bs]
        up_ref[i] = total[:, bs:]


def slot_grads(srow, scol, scale, tok_blocks, grads):
    cap = srow.shape[0]
    bs, tokens = tok_blocks.shape[1:]
    each = next(n for n in (4, 3, 2, 1) if cap % n == 0)
    return pl.pallas_call(
        slot_kernel,
        grid_spec=pltpu.PrefetchScalarGridSpec(
            num_scalar_prefetch=3,
            grid=(cap // each,),
            in_specs=[pl.BlockSpec(tok_blocks.shape, lambda s, *_: (0, 0, 0))]
            + [
                pl.BlockSpec((1, tokens, 2 * bs), lambda s, row, col, scale, i=i: (col[s * each + i], 0, 0))
                for i in range(each)
            ],
            out_specs=[pl.BlockSpec((each, bs, bs), lambda s, *_: (s, 0, 0))] * 2,
        ),
        out_shape=[jax.ShapeDtypeStruct((cap, bs, bs), jnp.float32)] * 2,
        compiler_params=pltpu.CompilerParams(vmem_limit_bytes=48 * 2**20),
        cost_estimate=pl.CostEstimate(
            flops=cap * tokens * bs * bs * 4, bytes_accessed=cap * tokens * bs * 4 + cap * bs * bs * 8, transcendentals=0
        ),
    )(srow, scol, scale, tok_blocks, *[grads] * each)


def on_device(layer_input, hidden_grad, gate_slots, up_slots, block_mask):
    gate_local, up_local = gate_slots[0, 0], up_slots[0, 0]
    local_cap, bs = gate_local.shape[0], gate_local.shape[-1]
    n_dp, n_row = lax.axis_size("dp"), lax.axis_size("row")
    feat = layer_input.shape[1]
    rows_each, units = hidden_grad.shape
    tile_rows, tile_cols = feat // bs, units // bs
    where_slot, srow, scol, live = slot_maps(block_mask, tile_rows, tile_cols, local_cap)
    scale = live.astype(jnp.float32) / n_dp
    tokens = lax.all_gather(layer_input, ("dp", "col"), axis=0, tiled=True)
    tokens = (
        tokens.reshape(n_dp, n_row, rows_each, feat).transpose(1, 0, 2, 3).reshape(n_row, n_dp * rows_each, feat)
    )
    weights = jnp.pad(jnp.concatenate([gate_local, up_local], axis=2), ((0, 1), (0, 0), (0, 0)))
    upstream = hidden_grad.reshape(rows_each, tile_cols, bs).transpose(1, 0, 2)
    lag = 2 if n_dp <= 4 else 1
    ring = 6 * lag + 2
    part_ring = lag + 1
    sizes = (n_row, n_dp, tile_cols, tile_rows, lag, ring, part_ring)
    wide = 2 * bs
    bf = jnp.bfloat16
    dma = pltpu.SemaphoreType.DMA
    vm = pl.BlockSpec(memory_space=pltpu.VMEM)
    sm = pl.BlockSpec(memory_space=pltpu.SMEM)
    dx, grads = pl.pallas_call(
        functools.partial(kernel, sizes),
        out_shape=(
            jax.ShapeDtypeStruct((n_row, n_dp * rows_each, feat), bf),
            jax.ShapeDtypeStruct((tile_cols, n_row, n_dp, rows_each, wide), bf),
        ),
        in_specs=[sm, vm, vm, vm],
        out_specs=(vm, pl.BlockSpec(memory_space=pl.ANY)),
        scratch_shapes=[
            pltpu.VMEM((tile_cols, n_row, n_dp, rows_each, wide), bf),
            pltpu.VMEM((part_ring, n_row, n_dp, rows_each, wide), bf),
            pltpu.VMEM((ring, 2, n_dp, rows_each, wide), bf),
            pltpu.VMEM((ring, n_dp, rows_each, wide), bf),
            pltpu.VMEM((ring, n_dp - 1, rows_each, wide), bf),
            pltpu.VMEM((feat, wide), bf),
            pltpu.VMEM((n_row, n_dp * rows_each, feat), jnp.float32),
            dma((ring, 2)), dma((ring, 2)),
            dma((ring,)), dma((ring,)),
            dma((ring, n_dp - 1)), dma((ring, n_dp - 1)),
            dma((ring, n_dp - 1)), dma((ring, n_dp - 1)),
            dma((ring,)), dma((ring,)),
            dma((ring, 2)), dma((ring, 2)),
            dma((tile_cols,)),
        ],
        compiler_params=pltpu.CompilerParams(
            collective_id=0, has_side_effects=True, vmem_limit_bytes=63 * 2**20
        ),
    )(where_slot, tokens, weights, upstream)
    dx = dx.reshape(n_row, n_dp, rows_each, feat).transpose(1, 0, 2, 3).reshape(-1, feat)
    tok_blocks = tokens.reshape(-1, tile_rows, bs).transpose(1, 2, 0)
    gate_out, up_out = slot_grads(srow, scol, scale, tok_blocks, grads.reshape(tile_cols, -1, wide))
    input_sum = lax.psum_scatter(dx, ("dp", "col"), scatter_dimension=0, tiled=True)
    return (input_sum, gate_out[None, None], up_out[None, None])


def solution(mesh):
    return jax.shard_map(
        on_device,
        mesh=mesh,
        in_specs=(
            P(("dp", "col"), "row"),
            P(("dp", "row"), "col"),
            P("row", "col", "dp", None, None),
            P("row", "col", "dp", None, None),
            P(),
        ),
        out_specs=(
            P(("dp", "col"), "row"),
            P("row", "col", "dp", None, None),
            P("row", "col", "dp", None, None),
        ),
        check_vma=False,
    )
```

time: 734 us -> 457 us (0.62)
  waiting for transfers between devices: 512 us -> 37.8 us
  Pallas kernels: 0 us -> 389 us
  matrix products: 154 us -> 0 us
  local copies, waits for them, and re-layouts: 30.5 us -> 11.1 us
  other arithmetic: 15.3 us -> 4.87 us
    pallas_call x0 -> x2, Pallas kernels: none -> 389 us  [the longest x1 374 us: on_device(): pl.pallas_call(functools.partial(kernel, sizes), out_shape=(jax.ShapeDtyp...]
    all_gather x3 -> x1, waiting for transfers between devices: 219 us -> 22.9 us  [on_device(): tokens = lax.all_gather(layer_input, ('dp', 'col'), axis=0, tiled=True)]
    dot_general x5 -> x0, matrix products: 154 us -> none  [the longest x1 67.1 us: slot_products(): jnp.einsum('tsn,sc->tcn', per_slot, col_table, precision=lax.Precision.HI...]
    reduce_scatter x2 -> x1, waiting for transfers between devices: 166 us -> 14.1 us  [on_device(): lax.psum_scatter(dx, ('dp', 'col'), scatter_dimension=0, tiled=True)]
    psum x1 -> x0, waiting for transfers between devices: 124 us -> none  [on_device(): lax.psum(gate_part.astype(jnp.bfloat16), 'row').astype(jnp.float32)]
    gather x2 -> x0, local copies, waits for them, and re-layouts: 22.8 us -> none  [the longest x1 12.9 us: on_device(): grad_picked = jnp.take(grad_pair, slot_col, axis=1)]
  transfers between devices with their start and end apart: 6 -> 2, of which waited for: 5 -> 2; matrix products, arithmetic and copies ran while one was open for 22% -> 2% of each run, Pallas kernels for 0% -> 3%
where the time goes in v1:
time: 457 us
  Pallas kernels  389 us (85%)
  waiting for transfers between devices  37.8 us (8%)
  between operations  14.1 us (3%)
  local copies, waits for them, and re-layouts  11.1 us (2%)
  other arithmetic  4.87 us (1%)
    pallas_call x1, Pallas kernels, on_device(): pl.pallas_call(functools.partial(kernel, sizes), out_shape=(jax.ShapeDtyp...  374 us
    all_gather x1, waiting for transfers between devices, on_device(): tokens = lax.all_gather(layer_input, ('dp', 'col'), axis=0, tiled=True)  22.9 us
    pallas_call x1, Pallas kernels, slot_grads(): pl.pallas_call(slot_kernel, grid_spec=pltpu.PrefetchScalarGridSpec(num_sc...  14.5 us
    reduce_scatter x1, waiting for transfers between devices, on_device(): lax.psum_scatter(dx, ('dp', 'col'), scatter_dimension=0, tiled=True)  14.1 us
  transfers between devices with their start and end apart: 2, of which 2 were waited for; matrix products, arithmetic and copies ran while one was open for 2% of the time, Pallas kernels for 3%

profile of v1, /device:TPU:0, one launch (start us, length us, event | category | flops | bytes accessed | tf_op | source)
XLA Modules:
  0.0 456.7 jit_solution(5332629947431985364)
XLA Ops:
  7.2 0.0 copy-start
  7.2 0.0 all-gather.2.cloned.1.call-start
  7.2 0.7 all-gather.2.cloned.1.call-update
  7.9 0.0 reduce-scatter.2.cloned.1.call-start
  8.0 0.8 dynamic_slice.3
  8.7 0.1 reshape.41
  8.8 0.1 select_reduce_fusion
  9.0 0.6 and_select_fusion.2.where_ref
  9.5 0.0 copy-done
  9.5 1.0 bitcast_bitcast_fusion.hg_ref
  10.5 4.0 fusion.2.w_ref
  14.5 22.9 %all-gather.2.cloned.1.call-done = bf16[768,1024]{1,0:T(8,128)(2,1)} async-done(((bf16[96,1024]{1,0:T(8,128)(2,1)}), bf16[768,1024]{1,0:T(8,128)(2,1)}) %all-gather.2.cloned.1.call-update) | async-done | bytes 1572880 | tf_op jit(solution)/shard_map/all_gather | solution.py:267
  37.4 2.7 copy.15
  40.2 374.3 %shard_map.76 = (bf16[4,192,1024]{2,1,0:T(8,128)(2,1)}, bf16[56,4,4,48,256]{4,3,2,1,0:T(8,128)(2,1)}) custom-call(s32[448]{0:T(512)} %and_select_fusion.2.where_ref, bf16[4,192,1024]{2,1,0:T(8,128)(2,1)} %bitcast.30, bf16[49,128,256]{2,1,0:T(8,128)(2,1)} %fusion.2.w_ref, bf16[56,48,128]{2,1,0:T(8,128)(2,1)} %bitcast_bitcast_fusion.hg_ref), custom_call_target="tpu_custom_call" | custom-call | tf_op jit(solution)/shard_map/pallas_call | solution.py:282
  414.5 0.0 copy-start.2
  414.5 0.0 copy-start.1
  414.5 2.9 copy.17
  417.4 0.0 reduce-scatter.2.cloned.1.call-update
  417.4 0.0 copy-done.2
  417.4 0.1 convert_reduce_fusion
  417.6 1.6 copy.20
  419.2 2.1 copy.18
  421.3 14.5 %shard_map.77 = (f32[48,128,128]{2,1,0:T(8,128)}, f32[48,128,128]{2,1,0:T(8,128)}) custom-call(s32[48]{0:T(128)S(1)} %get-tuple-element.14.srow_ref, s32[48]{0:T(128)S(1)} %get-tuple-element.13.scol_ref, f32[48]{0:T(128)S(1)} %convert_multiply_fusion.scale_ref, bf16[8,128,768]{2,1,0:T(8,128)(2,1)S(1)} %bitcast.25, bf16[56,768,256]{2,1,0:T(8,128)(2,1)} %bitcast.26, ...), custom_call_target="tpu_custom_call" | custom-call | flops 2415919104 | bytes 25165824 | tf_op jit(solution)/shard_map/pallas_call | solution.py:238
  435.8 14.1 %reduce-scatter.2.cloned.1.call-done = bf16[96,1024]{1,0:T(8,128)(2,1)} async-done(((bf16[768,1024]{1,0:T(8,128)(2,1)}), bf16[96,1024]{1,0:T(8,128)(2,1)}) %reduce-scatter.2.cloned.1.call-update) | async-done | bytes 196624 | tf_op jit(solution)/shard_map/reduce_scatter | solution.py:313
  (3 shorter events, 0.0 us)
Async XLA Ops:
  7.2 2.4 copy-start
  7.2 30.3 %all-gather.2.cloned.1.call-start = ((), (), s32[]{:S(2)}) async-start(), calls=%async_computation.1 | async-start | bytes 1769472 | tf_op jit(solution)/shard_map/all_gather | solution.py:267
  7.9 442.0 %reduce-scatter.2.cloned.1.call-start = ((), (), s32[]{:S(2)}) async-start(), calls=%async_computation.2 | async-start | bytes 1769472 | tf_op jit(solution)/shard_map/reduce_scatter | solution.py:313
  414.5 3.0 copy-start.2
  414.5 3.1 copy-start.1
Sparse Core Ops, SparseCore 0:
  9.7 27.7 all-gather.1
  417.5 32.2 reduce-scatter.1

commit v2 on v1

--- a/solution.py
+++ b/solution.py
@@ -186,7 +186,7 @@
 
             def rows(r, carry):
                 part[slot, r] = (
-                    jnp.dot(tok_ref[r], dense[...], preferred_element_type=jnp.float32)
+                    jnp.dot(tok_ref[:, r].reshape(-1, tok_ref.shape[-1]), dense[...], preferred_element_type=jnp.float32)
                     .astype(jnp.bfloat16)
                     .reshape(part.shape[2:])
                 )
@@ -208,7 +208,7 @@
     lax.fori_loop(0, n_chunks + 6 * lag, iteration, 0)
 
     def finish(r, carry):
-        dx_ref[r] = dx_acc[r].astype(jnp.bfloat16)
+        dx_ref[:, r] = dx_acc[r].astype(jnp.bfloat16).reshape(dx_ref.shape[:1] + dx_ref.shape[2:])
         return carry
 
     lax.fori_loop(0, n_row, finish, 0)
@@ -265,12 +265,10 @@
     where_slot, srow, scol, live = slot_maps(block_mask, tile_rows, tile_cols, local_cap)
     scale = live.astype(jnp.float32) / n_dp
     tokens = lax.all_gather(layer_input, ("dp", "col"), axis=0, tiled=True)
-    tokens = (
-        tokens.reshape(n_dp, n_row, rows_each, feat).transpose(1, 0, 2, 3).reshape(n_row, n_dp * rows_each, feat)
-    )
+    tokens = tokens.reshape(n_dp, n_row, rows_each, feat)
     weights = jnp.pad(jnp.concatenate([gate_local, up_local], axis=2), ((0, 1), (0, 0), (0, 0)))
     upstream = hidden_grad.reshape(rows_each, tile_cols, bs).transpose(1, 0, 2)
-    lag = 2 if n_dp <= 4 else 1
+    lag = 3 if n_dp <= 4 else 1
     ring = 6 * lag + 2
     part_ring = lag + 1
     sizes = (n_row, n_dp, tile_cols, tile_rows, lag, ring, part_ring)
@@ -282,7 +280,7 @@
     dx, grads = pl.pallas_call(
         functools.partial(kernel, sizes),
         out_shape=(
-            jax.ShapeDtypeStruct((n_row, n_dp * rows_each, feat), bf),
+            jax.ShapeDtypeStruct((n_dp, n_row, rows_each, feat), bf),
             jax.ShapeDtypeStruct((tile_cols, n_row, n_dp, rows_each, wide), bf),
         ),
         in_specs=[sm, vm, vm, vm],
@@ -307,10 +305,10 @@
             collective_id=0, has_side_effects=True, vmem_limit_bytes=63 * 2**20
         ),
     )(where_slot, tokens, weights, upstream)
-    dx = dx.reshape(n_row, n_dp, rows_each, feat).transpose(1, 0, 2, 3).reshape(-1, feat)
-    tok_blocks = tokens.reshape(-1, tile_rows, bs).transpose(1, 2, 0)
+    tok_blocks = tokens.reshape(n_dp, n_row, rows_each, tile_rows, bs).transpose(3, 4, 1, 0, 2)
+    tok_blocks = tok_blocks.reshape(tile_rows, bs, -1)
     gate_out, up_out = slot_grads(srow, scol, scale, tok_blocks, grads.reshape(tile_cols, -1, wide))
-    input_sum = lax.psum_scatter(dx, ("dp", "col"), scatter_dimension=0, tiled=True)
+    input_sum = lax.psum_scatter(dx.reshape(-1, feat), ("dp", "col"), scatter_dimension=0, tiled=True)
     return (input_sum, gate_out[None, None], up_out[None, None])
 
 

time: 457 us -> 449 us (0.982)
  transfers between devices with their start and end apart: 2 -> 2, of which waited for: 2 -> 2; matrix products, arithmetic and copies ran while one was open for 2% -> 3% of each run, Pallas kernels for 3% -> 3%
where the time goes in v2:
time: 449 us
  Pallas kernels  386 us (86%)
  waiting for transfers between devices  36.4 us (8%)
  between operations  14.1 us (3%)
  local copies, waits for them, and re-layouts  6.97 us (2%)
  other arithmetic  4.9 us (1%)
    pallas_call x1, Pallas kernels, on_device(): pl.pallas_call(functools.partial(kernel, sizes), out_shape=(jax.ShapeDtyp...  372 us
    all_gather x1, waiting for transfers between devices, on_device(): tokens = lax.all_gather(layer_input, ('dp', 'col'), axis=0, tiled=True)  22.9 us
    pallas_call x1, Pallas kernels, slot_grads(): pl.pallas_call(slot_kernel, grid_spec=pltpu.PrefetchScalarGridSpec(num_sc...  14.5 us
    reduce_scatter x1, waiting for transfers between devices, on_device(): lax.psum_scatter(dx.reshape(-1, feat), ('dp', 'col'), scatter_dimension=0...  12.8 us
  transfers between devices with their start and end apart: 2, of which 2 were waited for; matrix products, arithmetic and copies ran while one was open for 3% of the time, Pallas kernels for 3%

profile of v2, /device:TPU:0, one launch (start us, length us, event | category | flops | bytes accessed | tf_op | source)
XLA Modules:
  0.0 448.8 jit_solution(12785090587935630341)
XLA Ops:
  7.2 0.0 copy-start
  7.2 0.0 all-gather.2.cloned.1.call-start
  7.2 0.7 all-gather.2.cloned.1.call-update
  7.9 0.0 reduce-scatter.2.cloned.1.call-start
  8.0 0.8 dynamic_slice.3
  8.7 0.1 reshape.38
  8.8 0.1 select_reduce_fusion
  9.0 0.6 and_select_fusion.2.where_ref
  9.6 0.0 copy-done
  9.6 1.0 bitcast_bitcast_fusion.hg_ref
  10.5 4.0 fusion.2.w_ref
  14.5 22.9 %all-gather.2.cloned.1.call-done = bf16[768,1024]{1,0:T(8,128)(2,1)} async-done(((bf16[96,1024]{1,0:T(8,128)(2,1)}), bf16[768,1024]{1,0:T(8,128)(2,1)}) %all-gather.2.cloned.1.call-update) | async-done | bytes 1572880 | tf_op jit(solution)/shard_map/all_gather | solution.py:267
  37.4 0.0 copy-start.1
  37.4 371.9 %shard_map.76 = (bf16[4,4,48,1024]{3,2,1,0:T(8,128)(2,1)}, bf16[56,4,4,48,256]{4,3,2,1,0:T(8,128)(2,1)}) custom-call(s32[448]{0:T(512)} %and_select_fusion.2.where_ref, bf16[4,4,48,1024]{3,2,1,0:T(8,128)(2,1)} %bitcast.26, bf16[49,128,256]{2,1,0:T(8,128)(2,1)} %fusion.2.w_ref, bf16[56,48,128]{2,1,0:T(8,128)(2,1)} %bitcast_bitcast_fusion.hg_ref), custom_call_target="tpu_custom_call" | custom-call | tf_op jit(solution)/shard_map/pallas_call | solution.py:280
  409.3 0.0 reduce-scatter.2.cloned.1.call-update
  409.4 0.0 copy-done.1
  409.4 0.1 convert_reduce_fusion
  409.5 1.8 copy.18
  411.4 1.5 copy.15
  412.9 1.8 copy.16.tok_ref
  414.7 14.5 %shard_map.77 = (f32[48,128,128]{2,1,0:T(8,128)}, f32[48,128,128]{2,1,0:T(8,128)}) custom-call(s32[48]{0:T(128)S(1)} %get-tuple-element.14.srow_ref, s32[48]{0:T(128)S(1)} %get-tuple-element.13.scol_ref, f32[48]{0:T(128)S(1)} %convert_multiply_fusion.scale_ref, bf16[8,128,768]{2,1,0:T(8,128)(2,1)S(1)} %copy.16.tok_ref, bf16[56,768,256]{2,1,0:T(8,128)(2,1)} %bitcast.20, ...), custom_call_target="tpu_custom_call" | custom-call | flops 2415919104 | bytes 25165824 | tf_op jit(solution)/shard_map/pallas_call | solution.py:238
  429.2 12.8 %reduce-scatter.2.cloned.1.call-done = bf16[96,1024]{1,0:T(8,128)(2,1)} async-done(((bf16[768,1024]{1,0:T(8,128)(2,1)}), bf16[96,1024]{1,0:T(8,128)(2,1)}) %reduce-scatter.2.cloned.1.call-update) | async-done | bytes 196624 | tf_op jit(solution)/shard_map/reduce_scatter | solution.py:311
  (2 shorter events, 0.0 us)
Async XLA Ops:
  7.2 2.4 copy-start
  7.2 30.3 %all-gather.2.cloned.1.call-start = ((), (), s32[]{:S(2)}) async-start(), calls=%async_computation.1 | async-start | bytes 1769472 | tf_op jit(solution)/shard_map/all_gather | solution.py:267
  7.9 434.1 %reduce-scatter.2.cloned.1.call-start = ((), (), s32[]{:S(2)}) async-start(), calls=%async_computation.2 | async-start | bytes 1769472 | tf_op jit(solution)/shard_map/reduce_scatter | solution.py:311
  37.4 371.9 %copy-start.1 = (s32[448]{0:T(512)S(1)}, s32[448]{0:T(512)}, u32[]{:S(2)}) copy-start(s32[448]{0:T(512)} %and_select_fusion.2.where_ref) | copy-start | bytes 5380
Sparse Core Ops, SparseCore 0:
  9.7 27.7 all-gather.1
  409.5 32.4 reduce-scatter.1
